TPU v7x, 32 devices: a whole 2x2x4 slice. The times are simulated.
32 devices in a mesh: energy: 4 (over z), cluster: 2 (over x), tile: 4 (over y, core).
Axes of the slice: x: 2, y: 2, z: 4, core: 2. Of those that a mesh axis runs over, the one named last changes fastest.
Arguments:
- boundary: bfloat16 [2, 2, 512, 8, 2, 1024], P('cluster', None, 'tile', 'energy'), may hold values from -5 to 5
- column_source: int32 [2, 1024], P('cluster'), may hold values from 0 to 1023, as said below
- energy_weights: float32 [8], P('energy'), may hold values from 0.2 to 2
Outputs:
- final_rows: float32 [2, 512, 8, 2, 1024], P('cluster', 'tile', 'energy')
- density: float32 [2, 512], P('cluster', 'tile')
Inputs may be any that keep to these rules, and one draw needn't show every extreme that they name: `column_source`: for each cluster, every index 0 to 1023 appears once.
All inputs are finite; a program needn't handle non-finite values.
Results may differ from a plain program's by a relative error of at most 0.015.
Values may be sent and summed in bfloat16 or wider, within the bound.
A program may use at most 64 MiB of HBM per device.

v0:
```python
import jax
import jax.numpy as jnp
from jax import lax
from jax.sharding import PartitionSpec as P


def swapped(shard, axis, distance):
    return lax.ppermute(shard, axis, [(i, i ^ 1 << distance) for i in range(lax.axis_size(axis))])


def shortened(shard):
    return jax.tree.map(lambda a: a.astype(jnp.bfloat16) if a.dtype == jnp.float32 else a, shard)


def complex_product(left, right):

    def single(first_part, second_part):
        return jnp.einsum(
            "mek,ken->men", first_part, second_part, preferred_element_type=jnp.float32
        )

    real_part = single(left[:, :, 0], right[:, :, 0]) - single(left[:, :, 1], right[:, :, 1])
    imag_part = single(left[:, :, 0], right[:, :, 1]) + single(left[:, :, 1], right[:, :, 0])
    return jnp.stack([real_part, imag_part], axis=2)


def inverse_guess(interior):
    values = interior.astype(jnp.float32)
    diagonal = jnp.diagonal(values, axis1=0, axis2=3)
    denom = diagonal[:, 0] * diagonal[:, 0] + diagonal[:, 1] * diagonal[:, 1]
    inv_real = diagonal[:, 0] / denom
    inv_imag = -diagonal[:, 1] / denom
    column_real = inv_real[None, :, :]
    column_imag = inv_imag[None, :, :]
    row_real = inv_real.T[:, :, None]
    row_imag = inv_imag.T[:, :, None]
    values_real = values[:, :, 0]
    values_imag = values[:, :, 1]
    temp_real = values_real * column_real - values_imag * column_imag
    temp_imag = values_real * column_imag + values_imag * column_real
    prod_real = row_real * temp_real - row_imag * temp_imag
    prod_imag = row_real * temp_imag + row_imag * temp_real
    ident = jnp.eye(values.shape[0], dtype=jnp.float32)[:, None, :]
    guess_real = 2.0 * ident * row_real - prod_real
    guess_imag = 2.0 * ident * row_imag - prod_imag
    return jnp.stack([guess_real, guess_imag], axis=2).astype(jnp.bfloat16)


def place_block(block, is_low):
    zeros = jnp.zeros_like(block)
    return jnp.where(
        is_low, jnp.concatenate([block, zeros], axis=3), jnp.concatenate([zeros, block], axis=3)
    )


def swap_separator(separator, level_index):
    return swapped(separator, "cluster", level_index)


def eliminate(outer_coupling, start_block, interior, approx_inverse, coupling_rows):
    applied = complex_product(outer_coupling.astype(jnp.bfloat16), approx_inverse)
    middle = complex_product(applied.astype(jnp.bfloat16), interior).astype(jnp.bfloat16)
    reduced = (2.0 * applied - complex_product(middle, approx_inverse)).astype(jnp.bfloat16)
    row_piece = lax.all_gather(coupling_rows, "tile", axis=0, tiled=True)
    columns = lax.slice_in_dim(reduced, 0, row_piece.shape[0], axis=3)
    return start_block - complex_product(columns, row_piece)


def per_device(boundary, column_source, energy_weights):
    stored = boundary[0]
    canonical = jnp.take(stored, column_source[0], axis=4)
    separator = canonical[0]
    outer_rows = canonical[1]
    interior_width = separator.shape[3] // 2
    row_count = separator.shape[0]
    levels = min(2, lax.axis_size("cluster") // 2)
    cluster_index = lax.axis_index("cluster")
    tile_index = lax.axis_index("tile")
    for level_index in range(levels):
        side_bit = cluster_index // 2**level_index % 2
        is_low = side_bit == 0
        final_level = level_index == levels - 1
        if final_level:
            separator = separator.astype(jnp.float32)
            outer_rows = outer_rows.astype(jnp.float32)
            partner_outer = outer_rows
            partner_sep = swap_separator(separator, level_index)
        else:
            partner_sep, partner_outer = (
                swapped(shortened(separator), "cluster", level_index).astype(separator.dtype),
                swapped(shortened(outer_rows), "cluster", level_index).astype(outer_rows.dtype),
            )
            separator = separator.astype(jnp.float32)
            outer_rows = outer_rows.astype(jnp.float32)
            partner_sep = partner_sep.astype(jnp.float32)
            partner_outer = partner_outer.astype(jnp.float32)
        interior_rows = (
            separator[..., :interior_width] + partner_sep[..., :interior_width]
        ).astype(jnp.bfloat16)
        interior = lax.all_gather(interior_rows, "tile", axis=0, tiled=True)
        approx_inverse = inverse_guess(interior)
        low_sep = jnp.where(is_low, separator, partner_sep)
        high_sep = jnp.where(is_low, partner_sep, separator)
        coupling_rows = jnp.concatenate(
            [low_sep[..., interior_width:], high_sep[..., interior_width:]], axis=3
        ).astype(jnp.bfloat16)
        if final_level:
            share = row_count // 2**level_index
            within = cluster_index % 2**level_index
            own_rows = lax.dynamic_slice_in_dim(outer_rows, within * share, share, 0)
            new_rows = eliminate(
                own_rows[..., :interior_width],
                place_block(own_rows[..., interior_width:], is_low),
                interior,
                approx_inverse,
                coupling_rows,
            )
            columns = (
                side_bit * interior_width
                + tile_index * row_count
                + within * share
                + jnp.arange(share, dtype=jnp.int32)
            )
            selector = (
                jnp.arange(new_rows.shape[3], dtype=jnp.int32)[None, :] == columns[:, None]
            ).astype(jnp.float32)
            diagonal = jnp.sum(new_rows[:, :, 1, :] * selector[:, None, :], axis=2)
            partial_sum = jnp.sum(diagonal * energy_weights[None, :], axis=1)
            density = lax.psum(partial_sum, "energy")
            return (new_rows[None], density[None])
        else:
            low_outer = jnp.where(is_low, outer_rows, partner_outer)
            high_outer = jnp.where(is_low, partner_outer, outer_rows)
            outer_coupling = jnp.concatenate(
                [low_outer[..., :interior_width], high_outer[..., :interior_width]], axis=0
            )
            start_block = jnp.concatenate(
                [
                    place_block(low_outer[..., interior_width:], True),
                    place_block(high_outer[..., interior_width:], False),
                ],
                axis=0,
            )
            merged = eliminate(outer_coupling, start_block, interior, approx_inverse, coupling_rows)
            separator = merged[:row_count]
            outer_rows = merged[row_count:]


def solution(mesh):
    placed = (P("cluster", None, "tile", "energy", None, None), P("cluster", None), P("energy"))
    return jax.shard_map(
        per_device,
        mesh=mesh,
        in_specs=placed,
        out_specs=(P("cluster", "tile", "energy", None, None), P("cluster", "tile")),
        check_vma=False,
    )
```

profile of v0, /device:TPU:0, one launch (start us, length us, event | category | flops | bytes accessed | tf_op | source)
XLA Modules:
  0.0 174.4 jit_solution(11367060944980823916)
XLA Ops:
  7.2 0.0 all-gather.5.cloned.1.call-start
  7.2 8.9 %copy.77 = bf16[1,2,128,2,2,1024]{2,4,5,3,1,0:T(2,128)(2,1)S(1)} copy(bf16[1,2,128,2,2,1024]{5,4,3,2,1,0:T(2,128)(2,1)} %param.3) | data formatting | bytes 4194304 | tf_op args[0]
  16.2 12.1 %gather_fusion = bf16[1024,2,128,2,2]{2,4,3,1,0:T(2,128)(2,1)} fusion(bf16[2,128,2,2,1024]{1,3,4,2,0:T(2,128)(2,1)S(1)} %bitcast.140, s32[1024]{0:T(1024)S(1)} %broadcast_clamp_fusion), kind=kCustom, calls=%fused_computation | custom fusion | bytes 4198400 | tf_op jit(solution)/shard_map/jit(_take)/gather | solution.py:71
  28.3 4.7 %copy.78 = bf16[1024,2,128,2,2]{0,2,3,4,1:T(8,128)(2,1)S(1)} copy(bf16[1024,2,128,2,2]{2,4,3,1,0:T(2,128)(2,1)} %gather_fusion) | data formatting | bytes 4194304 | tf_op jit(solution)/shard_map/jit(_take)/gather | solution.py:71
  33.0 0.2 select_bitcast_fusion
  33.2 0.3 slice_bitcast_fusion.18
  33.5 3.0 %collective-permute-start = (f32[128,2,2,1024]{3,0,1,2:T(8,128)S(1)}, f32[128,2,2,1024]{3,0,1,2:T(8,128)S(1)}, u32[]{:S(2)}, u32[]{:S(2)}) collective-permute-start(f32[128,2,2,1024]{3,0,1,2:T(8,128)S(1)} %get-tuple-element.13), channel_id=1, source_target_pairs={{0,4},{4,0},{1,5},{5,1},{2,6},{6,2},{3,7},{7,3},{8,12},{12,8},{9,1... | collective-permute-start | bytes 6291464 | tf_op jit(solution)/shard_map/ppermute | solution.py:8
  36.5 45.6 %collective-permute-done = f32[128,2,2,1024]{3,0,1,2:T(8,128)S(1)} collective-permute-done((f32[128,2,2,1024]{3,0,1,2:T(8,128)S(1)}, f32[128,2,2,1024]{3,0,1,2:T(8,128)S(1)}, u32[]{:S(2)}, u32[]{:S(2)}) %collective-permute-start) | collective-permute-done | bytes 2097184 | tf_op jit(solution)/shard_map/ppermute | solution.py:8
  82.2 1.3 copy-done.4
  83.5 1.0 fusion.20
  84.5 0.0 all-gather.3.cloned.1.call-start
  84.5 1.7 select_convert_fusion.1
  86.2 1.1 pad_maximum_fusion
  87.4 0.1 fusion.23
  87.5 0.9 fusion.27
  88.4 0.1 slice_convert_fusion
  88.5 20.2 %all-gather.5.cloned.1.call-done = bf16[512,2,2,512]{3,0,1,2:T(8,128)(2,1)} async-done(((bf16[128,2,2,512]{3,0,1,2:T(8,128)(2,1)}), bf16[512,2,2,512]{3,0,1,2:T(8,128)(2,1)}) %all-gather.5.cloned.1.call-update) | async-done | bytes 2097168 | tf_op jit(solution)/shard_map/all_gather | solution.py:100
  108.7 4.2 %fusion.31 = (f32[512,2,2,512]{3,0,1,2:T(8,128)}, f32[2,2,512,512]{3,2,0,1:T(8,128)S(1)}) fusion(bf16[512,2,2,512]{3,0,1,2:T(8,128)(2,1)} %all-gather.5.cloned.1.call-done), kind=kLoop, calls=%fused_computation.80 | loop fusion | flops 1048576 | bytes 10485760 | tf_op jit(solution)/shard_map/convert_element_type | solution.py:28
  112.9 5.2 %copy.79 = f32[2,2,512,512]{3,1,2,0:T(2,128)} copy(f32[2,2,512,512]{3,2,0,1:T(8,128)S(1)} %get-tuple-element.15) | data formatting | bytes 8388608 | tf_op jit(solution)/shard_map/jit(diagonal)/transpose | solution.py:29
  118.1 7.0 %gather_fusion.1 = f32[512,2,2]{0,2,1:T(2,128)S(1)} fusion(f32[2,2,512,512]{3,1,2,0:T(2,128)} %copy.79, s32[512]{0:T(512)S(1)} %bitcast.139), kind=kCustom, calls=%fused_computation.1 | custom fusion | bytes 20480 | tf_op jit(solution)/shard_map/jit(diagonal)/gather | solution.py:29
  125.2 2.8 %fusion.16 = (bf16[512,2,512]{2,0,1:T(8,128)(2,1)S(1)}, bf16[512,2,512]{2,0,1:T(8,128)(2,1)S(1)}) fusion(f32[512,2]{0,1:T(2,128)S(1)} %bitcast.142, f32[512,2]{0,1:T(2,128)S(1)} %bitcast.141, f32[512,512]{1,0:T(8,128)S(1)} %fusion.23, f32[2,512]{1,0:T(2,128)S(1)} %get-tuple-element.17, f32[512,2,2,512]{3,0,1,2:T(8,128)} %get-tuple-element.14, ...), kind=kLoop, calls=%fused_computation.32 | loop fusion | flops 9437184 | bytes 7356416 | tf_op jit(solution)/shard_map/squeeze | solution.py:22
  128.1 0.5 fusion.29
  128.6 0.5 fusion.11
  129.1 0.5 fusion.28
  129.7 0.5 fusion.10
  130.2 0.1 fusion.26
  130.3 1.0 copy-done
  131.3 0.5 fusion.24
  131.8 0.5 fusion.15
  132.3 0.5 fusion.33
  132.8 0.5 fusion.25
  133.4 0.5 fusion.14
  133.9 0.5 fusion.9
  134.4 0.5 fusion.34
  135.0 0.5 fusion.8
  135.5 0.1 fusion.22
  135.6 9.7 %all-gather.3.cloned.1.call-done = bf16[512,2,2,1024]{3,0,1,2:T(8,128)(2,1)} async-done(((bf16[128,2,2,1024]{3,0,1,2:T(8,128)(2,1)}), bf16[512,2,2,1024]{3,0,1,2:T(8,128)(2,1)}) %all-gather.3.cloned.1.call-update) | async-done | bytes 4194320 | tf_op jit(solution)/shard_map/all_gather | solution.py:64
  145.4 2.2 %fusion.1 = f32[2,1024,128]{1,2,0:T(8,128)S(1)} fusion(bf16[512,2,2,1024]{3,0,1,2:T(8,128)(2,1)} %all-gather.3.cloned.1.call-done, bf16[128,2,2,512]{0,3,1,2:T(8,128)(2,1)S(1)} %fusion.22), kind=kOutput, calls=%fused_computation.11 | convolution fusion | flops 268435456 | bytes 3407872 | tf_op jit(solution)/shard_map/mek,ken->men/dot_general | solution.py:18
  147.6 2.1 %fusion = f32[2,1024,128]{1,2,0:T(8,128)S(1)} fusion(bf16[512,2,2,1024]{3,0,1,2:T(8,128)(2,1)} %all-gather.3.cloned.1.call-done, bf16[128,2,2,512]{0,3,1,2:T(8,128)(2,1)S(1)} %fusion.22), kind=kOutput, calls=%fused_computation.10 | convolution fusion | flops 268435456 | bytes 3407872 | tf_op jit(solution)/shard_map/mek,ken->men/dot_general | solution.py:18
  149.7 0.5 fusion.5
  150.2 0.5 fusion.7
  150.7 0.5 maximum_subtract_fusion
  151.2 0.5 fusion.47
  151.7 0.6 copy-done.3
  152.2 0.2 fusion.19
  152.4 0.1 multiply_reduce_fusion
  152.5 12.2 %psum.7 = f32[1,128]{1,0:T(1,128)} all-reduce(f32[1,128]{1,0:T(1,128)S(1)} %bitcast.146), channel_id=1, replica_groups=mesh['energy'=4,'cluster'=2,'tile'=4] {'energy'}, use_global_device_ids=true, to_apply=%region_2.3 | all-reduce | flops 128 | bytes 1024 | tf_op jit(solution)/shard_map/psum | solution.py:129
  164.7 2.9 %copy.115 = f32[1,128,2,2,1024]{4,3,2,1,0:T(2,128)} copy(f32[1,128,2,2,1024]{4,1,2,3,0:T(8,128)S(1)} %fusion.47) | data formatting | bytes 4194304
  (20 shorter events, 0.1 us)
Async XLA Ops:
  7.2 9.0 %copy-start.5 = (s32[1,1024]{1,0:T(1,128)S(1)}, s32[1,1024]{1,0:T(1,128)}, u32[]{:S(2)}) copy-start(s32[1,1024]{1,0:T(1,128)} %param.4) | copy-start | bytes 12292
  7.2 101.5 %all-gather.5.cloned.1.call-start = ((), (), s32[]{:S(2)}) async-start(), calls=%async_computation.1 | async-start | bytes 2621440 | tf_op jit(solution)/shard_map/all_gather | solution.py:100
  33.5 48.6 %copy-start.1 = (f32[128,2,2,1024]{3,0,1,2:T(8,128)}, f32[128,2,2,1024]{3,0,1,2:T(8,128)S(1)}, u32[]{:S(2)}) copy-start(f32[128,2,2,1024]{3,0,1,2:T(8,128)S(1)} %get-tuple-element.13) | copy-start | bytes 6291460
  33.5 48.6 %collective-permute-start = (f32[128,2,2,1024]{3,0,1,2:T(8,128)S(1)}, f32[128,2,2,1024]{3,0,1,2:T(8,128)S(1)}, u32[]{:S(2)}, u32[]{:S(2)}) collective-permute-start(f32[128,2,2,1024]{3,0,1,2:T(8,128)S(1)} %get-tuple-element.13), channel_id=1, source_target_pairs={{0,4},{4,0},{1,5},{5,1},{2,6},{6,2},{3,7},{7,3},{8,12},{12,8},{9,1... | collective-permute-start | bytes 6291464 | tf_op jit(solution)/shard_map/ppermute | solution.py:8
  82.2 1.3 copy-start.4
  84.5 60.9 %all-gather.3.cloned.1.call-start = ((), (), s32[]{:S(2)}) async-start(), calls=%async_computation | async-start | bytes 5242880 | tf_op jit(solution)/shard_map/all_gather | solution.py:64
  129.7 1.6 copy-start
  145.4 4.3 %copy-start.2 = (bf16[512,2,2,1024]{3,0,1,2:T(8,128)(2,1)S(1)}, bf16[512,2,2,1024]{3,0,1,2:T(8,128)(2,1)}, u32[]{:S(2)}) copy-start(bf16[512,2,2,1024]{3,0,1,2:T(8,128)(2,1)} %all-gather.3.cloned.1.call-done) | copy-start | bytes 12582916
  151.2 1.0 copy-start.3
  151.2 1.2 copy-start.6
Sparse Core Ops, SparseCore 0:
  84.6 24.0 all-gather.4
  110.8 34.4 all-gather.2
where the time goes:
time: 175 us; the launch traced here: 174 us
  waiting for transfers between devices  75.6 us (43%)
  local copies, waits for them, and re-layouts  43.8 us (25%)
  between operations  14.4 us (8%)
  other arithmetic  13.8 us (8%)
  blocking collectives  12.2 us (7%)
  matrix products  11.7 us (7%)
  starting transfers between devices  3.08 us (2%)
    ppermute x1, waiting for transfers between devices, swapped(): lax.ppermute(shard, axis, [(i, i ^ 1 << distance) for i in range(lax.axis...  45.6 us
    all_gather x1, waiting for transfers between devices, per_device(): interior = lax.all_gather(interior_rows, 'tile', axis=0, tiled=True)  20.2 us
    gather x2, local copies, waits for them, and re-layouts, per_device(): canonical = jnp.take(stored, column_source[0], axis=4)  16.8 us
    unnamed x16, local copies, waits for them, and re-layouts  14.7 us
    psum x1, blocking collectives, per_device(): density = lax.psum(partial_sum, 'energy')  12.2 us
    dot_general x16, matrix products, single(): jnp.einsum('mek,ken->men', first_part, second_part, preferred_element_typ...  11.7 us
    all_gather x1, waiting for transfers between devices, eliminate(): row_piece = lax.all_gather(coupling_rows, 'tile', axis=0, tiled=True)  9.72 us
    gather x1, local copies, waits for them, and re-layouts, inverse_guess(): diagonal = jnp.diagonal(values, axis1=0, axis2=3)  7.05 us
  transfers between devices with their start and end apart: 3, of which 3 were waited for; matrix products, arithmetic and copies ran while one was open for 17% of the time, Pallas kernels for 0%

commit v1 on v0

--- a/solution.py
+++ b/solution.py
@@ -1,6 +1,10 @@
+import functools
+
 import jax
 import jax.numpy as jnp
 from jax import lax
+from jax.experimental import pallas as pl
+from jax.experimental.pallas import tpu as pltpu
 from jax.sharding import PartitionSpec as P
 
 
@@ -26,7 +30,8 @@
 
 def inverse_guess(interior):
     values = interior.astype(jnp.float32)
-    diagonal = jnp.diagonal(values, axis1=0, axis2=3)
+    same = jnp.eye(values.shape[0], dtype=jnp.float32)[:, None, None, :]
+    diagonal = jnp.sum(values * same, axis=0)
     denom = diagonal[:, 0] * diagonal[:, 0] + diagonal[:, 1] * diagonal[:, 1]
     inv_real = diagonal[:, 0] / denom
     inv_imag = -diagonal[:, 1] / denom
@@ -66,9 +71,16 @@
     return start_block - complex_product(columns, row_piece)
 
 
+def permuted(stored, source):
+    nodes = jnp.arange(stored.shape[-1], dtype=jnp.int32)
+    picks = (nodes[:, None] == source[None, :]).astype(jnp.bfloat16)
+    picked = jnp.einsum("...j,jm->...m", stored, picks, preferred_element_type=jnp.float32)
+    return picked.astype(jnp.bfloat16)
+
+
 def per_device(boundary, column_source, energy_weights):
     stored = boundary[0]
-    canonical = jnp.take(stored, column_source[0], axis=4)
+    canonical = permuted(stored, column_source[0])
     separator = canonical[0]
     outer_rows = canonical[1]
     interior_width = separator.shape[3] // 2
@@ -146,10 +158,355 @@
             outer_rows = merged[row_count:]
 
 
+LANES = 128
+
+
+def dot(first, second):
+    return jnp.dot(first, second, preferred_element_type=jnp.float32)
+
+
+def complex_rows(stacked, real, imag):
+    rows = stacked.shape[0] // 2
+    by_real, by_imag = dot(stacked, real), dot(stacked, imag)
+    return by_real[:rows] - by_imag[rows:], by_imag[:rows] + by_real[rows:]
+
+
+def stack_rows(real, imag):
+    return jnp.concatenate([real.astype(jnp.bfloat16), imag.astype(jnp.bfloat16)], axis=0)
+
+
+def guess_of(real, imag):
+    size = real.shape[0]
+    step = min(128, size)
+    ident = (
+        lax.broadcasted_iota(jnp.int32, (step, step), 0)
+        == lax.broadcasted_iota(jnp.int32, (step, step), 1)
+    )
+
+    def inverse_of(axis):
+        def diagonal(values):
+            cuts = [
+                jnp.sum(
+                    jnp.where(ident, values[b : b + step, b : b + step], 0.0),
+                    axis=axis,
+                    keepdims=True,
+                )
+                for b in range(0, size, step)
+            ]
+            return jnp.concatenate(cuts, axis=1 - axis)
+
+        diag_real, diag_imag = diagonal(real), diagonal(imag)
+        denom = diag_real * diag_real + diag_imag * diag_imag
+        return diag_real / denom, -diag_imag / denom
+
+    column_real, column_imag = inverse_of(0)
+    row_real, row_imag = inverse_of(1)
+    temp_real = real * column_real - imag * column_imag
+    temp_imag = real * column_imag + imag * column_real
+    prod_real = row_real * temp_real - row_imag * temp_imag
+    prod_imag = row_real * temp_imag + row_imag * temp_real
+    whole = (
+        lax.broadcasted_iota(jnp.int32, real.shape, 0)
+        == lax.broadcasted_iota(jnp.int32, real.shape, 1)
+    )
+    guess_real = jnp.where(whole, 2.0 * row_real, 0.0) - prod_real
+    guess_imag = jnp.where(whole, 2.0 * row_imag, 0.0) - prod_imag
+    return guess_real.astype(jnp.bfloat16), guess_imag.astype(jnp.bfloat16)
+
+
+def merge_kernel(
+    n_energy,
+    boundary,
+    source,
+    weights,
+    out,
+    density,
+    raw,
+    picks,
+    flat,
+    outer,
+    own_sep,
+    peer_sep,
+    inner,
+    right,
+    inverse,
+    columns,
+    terms,
+    load_sem,
+    store_sem,
+    send_sem,
+    recv_sem,
+    term_send,
+    term_recv,
+):
+    _, rows, energies, _, width = boundary.shape
+    half = width // 2
+    lines = rows * energies * 2
+    every = energies * 2
+    blocks = half // LANES
+
+    def put(buffer, value, first=0):
+        for block in range(blocks):
+            buffer[first + block] = value[:, block * LANES : (block + 1) * LANES]
+
+    def get(buffer, e, part, first=0):
+        line = pl.ds(2 * e + part, rows, stride=every)
+        return jnp.concatenate([buffer[first + b, line, :] for b in range(blocks)], axis=1)
+
+    def scatter(buffer, e, part, value):
+        line = pl.ds(2 * e + part, rows, stride=every)
+        for block in range(blocks):
+            buffer[block, line, :] = value[:, block * LANES : (block + 1) * LANES]
+
+    cluster = lax.axis_index("cluster")
+    tile = lax.axis_index("tile")
+    energy = lax.axis_index("energy")
+    over = 1 - cluster
+    core = lax.rem(tile, 2)
+    level = tile // 2
+    beside = level * 2 + (1 - core)
+    across = (1 - level) * 2 + core
+    to_x, to_y, to_core = {"cluster": over}, {"tile": across}, {"tile": beside}
+
+    loads = [
+        pltpu.make_async_copy(
+            boundary.at[part].reshape(lines, width), raw.at[part], load_sem.at[part]
+        )
+        for part in range(2)
+    ]
+    for load in loads:
+        load.start()
+    barrier = pltpu.get_barrier_semaphore()
+    for there in (to_x, to_y, to_core):
+        pl.semaphore_signal(barrier, inc=1, device_id=there, device_id_type=pl.DeviceIdType.MESH)
+    for step in range(1, n_energy):
+        pl.semaphore_signal(
+            barrier,
+            inc=1,
+            device_id={"energy": lax.rem(energy + step, n_energy)},
+            device_id_type=pl.DeviceIdType.MESH,
+        )
+
+    wanted = source[...]
+    deep = min(256, width)
+    for begin in range(0, width, deep):
+        node = lax.broadcasted_iota(jnp.int32, (deep, width), 0) + begin
+        picks[begin : begin + deep, :] = jnp.where(node == wanted, 1.0, 0.0).astype(jnp.bfloat16)
+    loads[0].wait()
+    pl.semaphore_wait(barrier, 2 + n_energy)
+
+    def rows_of(which):
+        return pl.ds(pl.multiple_of(which * rows, rows), rows)
+
+    def send(kind, e, src, dst, there):
+        copy = pltpu.make_async_remote_copy(
+            src_ref=src,
+            dst_ref=dst,
+            send_sem=send_sem.at[kind, e],
+            recv_sem=recv_sem.at[kind, e],
+            device_id=there,
+            device_id_type=pl.DeviceIdType.MESH,
+        )
+        copy.start()
+        copies[kind, e] = copy
+
+    def pass_on(kind, e, ref, there):
+        send(kind, e, ref, ref, there)
+
+    def right_at(which, e, block):
+        return right.at[which, e, :, rows_of(block), :]
+
+    def inner_at(e, block):
+        return inner.at[e, :, rows_of(block), :]
+
+    copies = {}
+    sep_x, so_x, so_y, in_y, diag = range(5)
+    core_in, core_in_y, core_so, core_so_y, core_so_x, core_diag = range(5, 11)
+    all_e = list(range(energies))
+    by_x = energies // 2
+
+    put(flat, dot(raw[0], picks[:, :half]))
+    for e in all_e:
+        for part in range(2):
+            own_sep[e, part] = get(flat, e, part).astype(jnp.bfloat16)
+        send(sep_x, e, own_sep.at[e], peer_sep.at[e], to_x)
+    put(flat, dot(raw[0], picks[:, half:]))
+    for e in all_e:
+        for part in range(2):
+            right[cluster, e, part, rows_of(tile), :] = get(flat, e, part).astype(jnp.bfloat16)
+        pass_on(so_y, e, right_at(cluster, e, tile), to_y)
+    for e in reversed(all_e):
+        pass_on(so_x, e, right_at(cluster, e, tile), to_x)
+    for e in all_e:
+        pass_on(core_so, e, right_at(cluster, e, tile), to_core)
+
+    loads[1].wait()
+    put(outer, dot(raw[1], picks[:, :half]))
+    put(outer, dot(raw[1], picks[:, half:]), blocks)
+
+    for e in all_e:
+        copies[sep_x, e].wait_recv()
+        for part in range(2):
+            inner[e, part, rows_of(tile), :] = (
+                own_sep[e, part].astype(jnp.float32) + peer_sep[e, part].astype(jnp.float32)
+            ).astype(jnp.bfloat16)
+        pass_on(in_y, e, inner_at(e, tile), to_y)
+        pass_on(core_in, e, inner_at(e, tile), to_core)
+        copies[so_y, e].wait_recv()
+        if e < by_x:
+            pass_on(diag, e, right_at(cluster, e, across), to_x)
+        pass_on(core_so_y, e, right_at(cluster, e, across), to_core)
+
+    def take_x(e):
+        copies[so_x, e].wait_recv()
+        if e >= by_x:
+            pass_on(diag, e, right_at(over, e, tile), to_y)
+        pass_on(core_so_x, e, right_at(over, e, tile), to_core)
+
+    def take_inner(e):
+        copies[in_y, e].wait_recv()
+        pass_on(core_in_y, e, inner_at(e, across), to_core)
+
+    for e, x in zip(all_e, reversed(all_e)):
+        take_inner(e)
+        take_x(x)
+        copies[core_in, e].wait_recv()
+        copies[core_in_y, e].wait_recv()
+        guess_real, guess_imag = guess_of(
+            inner[e, 0].astype(jnp.float32), inner[e, 1].astype(jnp.float32)
+        )
+        inverse[0] = guess_real
+        inverse[1] = guess_imag
+        left = stack_rows(get(outer, e, 0), get(outer, e, 1))
+        applied_real, applied_imag = complex_rows(left, inverse[0], inverse[1])
+        middle = stack_rows(
+            *complex_rows(stack_rows(applied_real, applied_imag), inner[e, 0], inner[e, 1])
+        )
+        again_real, again_imag = complex_rows(middle, inverse[0], inverse[1])
+        columns[e] = stack_rows(2.0 * applied_real - again_real, 2.0 * applied_imag - again_imag)
+
+    for e in all_e:
+        copies[core_so, e].wait_recv()
+        copies[core_so_y, e].wait_recv()
+    wide = out.reshape(lines, width)
+
+    def store(buffer, block, which):
+        column = pl.multiple_of(which * half + block * LANES, LANES)
+        copy = pltpu.make_async_copy(
+            buffer.at[block], wide.at[:, pl.ds(column, LANES)], store_sem.at[which, block]
+        )
+        copy.start()
+        return copy
+
+    ident = lax.broadcasted_iota(jnp.int32, (rows, rows), 0) == lax.broadcasted_iota(
+        jnp.int32, (rows, rows), 1
+    )
+    partial = jnp.zeros((1, rows), jnp.float32)
+    for e in all_e:
+        real, imag = complex_rows(columns[e], right[cluster, e, 0], right[cluster, e, 1])
+        scatter(flat, e, 0, get(outer, e, 0, blocks) - real)
+        imag = get(outer, e, 1, blocks) - imag
+        scatter(flat, e, 1, imag)
+        corner = jnp.zeros((rows, rows), jnp.float32)
+        for which in range(half // rows):
+            chosen = ident & (tile == which)
+            corner = corner + jnp.where(chosen, imag[:, which * rows : (which + 1) * rows], 0.0)
+        partial = partial + weights[e] * jnp.sum(corner, axis=0, keepdims=True)
+    stores = [store(flat, block, cluster) for block in range(blocks)]
+    terms[energy] = jnp.broadcast_to(partial, terms.shape[1:])
+    swaps = []
+    for step in range(1, n_energy):
+        swap = pltpu.make_async_remote_copy(
+            src_ref=terms.at[energy],
+            dst_ref=terms.at[energy],
+            send_sem=term_send.at[step],
+            recv_sem=term_recv.at[step],
+            device_id={"energy": lax.rem(energy + step, n_energy)},
+            device_id_type=pl.DeviceIdType.MESH,
+        )
+        swap.start()
+        swaps.append(swap)
+
+    for e in all_e:
+        copies[diag, e].wait_recv()
+        pass_on(core_diag, e, right_at(over, e, across), to_core)
+    pair = 2 * rows
+    here = pl.ds(pl.multiple_of(level * pair, pair), pair)
+    there = pl.ds(pl.multiple_of((1 - level) * pair, pair), pair)
+
+    def far_part(e, band):
+        return complex_rows(
+            columns[e, :, band], right[over, e, 0, band, :], right[over, e, 1, band, :]
+        )
+
+    for e in all_e:
+        copies[core_so_x, e].wait_recv()
+        real, imag = far_part(e, here)
+        scatter(outer, e, 0, -real)
+        scatter(outer, e, 1, -imag)
+    for e in all_e:
+        copies[core_diag, e].wait_recv()
+        real, imag = far_part(e, there)
+        scatter(outer, e, 0, get(outer, e, 0) - real)
+        scatter(outer, e, 1, get(outer, e, 1) - imag)
+    stores += [store(outer, block, over) for block in range(blocks)]
+    for swap in swaps:
+        swap.wait()
+    density[...] = jnp.sum(terms[...], axis=0)[:1]
+    for copy in copies.values():
+        copy.wait_send()
+    for copy in stores:
+        copy.wait()
+
+
+def merge_once(boundary, column_source, energy_weights):
+    _, _, rows, energies, _, width = boundary.shape
+    half = width // 2
+    lines = rows * energies * 2
+    n_energy = lax.axis_size("energy")
+    n_tile = lax.axis_size("tile")
+    bf16, f32 = jnp.bfloat16, jnp.float32
+    anywhere = pl.BlockSpec(memory_space=pl.ANY)
+    vmem = pl.BlockSpec(memory_space=pltpu.VMEM)
+    result, density = pl.pallas_call(
+        functools.partial(merge_kernel, n_energy),
+        out_shape=(
+            jax.ShapeDtypeStruct((rows, energies, 2, width), f32),
+            jax.ShapeDtypeStruct((1, rows), f32),
+        ),
+        in_specs=[anywhere, vmem, pl.BlockSpec(memory_space=pltpu.SMEM)],
+        out_specs=(anywhere, vmem),
+        scratch_shapes=[
+            pltpu.VMEM((2, lines, width), bf16),
+            pltpu.VMEM((width, width), bf16),
+            pltpu.VMEM((half // LANES, lines, LANES), f32),
+            pltpu.VMEM((width // LANES, lines, LANES), f32),
+            pltpu.VMEM((energies, 2, rows, half), bf16),
+            pltpu.VMEM((energies, 2, rows, half), bf16),
+            pltpu.VMEM((energies, 2, half, half), bf16),
+            pltpu.VMEM((2, energies, 2, half, half), bf16),
+            pltpu.VMEM((2, half, half), bf16),
+            pltpu.VMEM((energies, 2 * rows, half), bf16),
+            pltpu.VMEM((n_energy, 8, rows), f32),
+            pltpu.SemaphoreType.DMA((2,)),
+            pltpu.SemaphoreType.DMA((2, half // LANES)),
+            pltpu.SemaphoreType.DMA((11, energies)),
+            pltpu.SemaphoreType.DMA((11, energies)),
+            pltpu.SemaphoreType.DMA((n_energy,)),
+            pltpu.SemaphoreType.DMA((n_energy,)),
+        ],
+        compiler_params=pltpu.CompilerParams(
+            collective_id=0, has_side_effects=True, vmem_limit_bytes=48 << 20
+        ),
+    )(boundary[0], column_source, energy_weights)
+    return result[None], density
+
+
 def solution(mesh):
     placed = (P("cluster", None, "tile", "energy", None, None), P("cluster", None), P("energy"))
+    paired = mesh.shape["cluster"] == 2 and mesh.shape["tile"] == 4
     return jax.shard_map(
-        per_device,
+        merge_once if paired else per_device,
         mesh=mesh,
         in_specs=placed,
         out_specs=(P("cluster", "tile", "energy", None, None), P("cluster", "tile")),

time: 175 us -> 47 us (0.27)
  waiting for transfers between devices: 75.6 us -> 0 us
  Pallas kernels: 0 us -> 41.4 us
  local copies, waits for them, and re-layouts: 43.8 us -> 4.76 us
  other arithmetic: 13.8 us -> 0 us
  between operations: 14.4 us -> 0.65 us
  blocking collectives: 12.2 us -> 0 us
  matrix products: 11.7 us -> 0 us
  starting transfers between devices: 3.08 us -> 0 us
    ppermute x1 -> x0, waiting for transfers between devices: 45.6 us -> none  [swapped(): lax.ppermute(shard, axis, [(i, i ^ 1 << distance) for i in range(lax.axis...]
    pallas_call x0 -> x1, Pallas kernels: none -> 41.4 us  [merge_once(): pl.pallas_call(functools.partial(merge_kernel, n_energy), out_shape=(jax....]
    all_gather x2 -> x0, waiting for transfers between devices: 29.9 us -> none  [the longest x1 20.2 us: per_device(): interior = lax.all_gather(interior_rows, 'tile', axis=0, tiled=True)]
    gather x3 -> x0, local copies, waits for them, and re-layouts: 23.8 us -> none  [the longest x2 16.8 us: per_device(): canonical = jnp.take(stored, column_source[0], axis=4)]
    psum x1 -> x0, blocking collectives: 12.2 us -> none  [per_device(): density = lax.psum(partial_sum, 'energy')]
    dot_general x16 -> x0, matrix products: 11.7 us -> none  [single(): jnp.einsum('mek,ken->men', first_part, second_part, preferred_element_typ...]
    unnamed x16 -> x8, local copies, waits for them, and re-layouts: 14.7 us -> 4.76 us
    convert_element_type x6 -> x0, other arithmetic: 6.54 us -> none  [the longest x1 4.21 us: inverse_guess(): values = interior.astype(jnp.float32)]
  transfers between devices with their start and end apart: 3 -> 0, of which waited for: 3 -> 0; matrix products, arithmetic and copies ran while one was open for 17% -> 0% of each run, Pallas kernels for 0% -> 0%
where the time goes in v1:
time: 47 us; the launch traced here: 46.8 us
  Pallas kernels  41.4 us (88%)
  local copies, waits for them, and re-layouts  4.76 us (10%)
  between operations  0.65 us (1%)
    pallas_call x1, Pallas kernels, merge_once(): pl.pallas_call(functools.partial(merge_kernel, n_energy), out_shape=(jax....  41.4 us
    unnamed x8, local copies, waits for them, and re-layouts  4.76 us

profile of v1, /device:TPU:0, one launch (start us, length us, event | category | flops | bytes accessed | tf_op | source)
XLA Modules:
  0.0 46.8 jit_solution(9280285672163278530)
XLA Ops:
  0.6 0.0 copy-start
  0.6 1.6 %copy-done = bf16[1,2,128,2,2,1024]{5,4,3,2,1,0:T(2,128)(2,1)S(1)} copy-done((bf16[1,2,128,2,2,1024]{5,4,3,2,1,0:T(2,128)(2,1)S(1)}, bf16[1,2,128,2,2,1024]{5,4,3,2,1,0:T(2,128)(2,1)}, u32[]{:S(2)}) %copy-start) | copy-done | bytes 2097176
  2.2 0.0 copy-start.1
  2.2 0.7 %copy-done.1 = s32[1,1024]{1,0:T(1,128)S(1)} copy-done((s32[1,1024]{1,0:T(1,128)S(1)}, s32[1,1024]{1,0:T(1,128)}, u32[]{:S(2)}) %copy-start.1) | copy-done | bytes 4120
  2.9 0.0 copy-start.2
  2.9 0.7 %copy-done.2 = f32[2]{0:T(128)S(1)} copy-done((f32[2]{0:T(128)S(1)}, f32[2]{0:T(128)}, u32[]{:S(2)}) %copy-start.2) | copy-done | bytes 32
  3.6 41.4 %shard_map.50 = (f32[128,2,2,1024]{3,2,1,0:T(2,128)S(1)}, f32[1,128]{1,0:T(1,128)S(1)}) custom-call(bf16[2,128,2,2,1024]{4,3,2,1,0:T(2,128)(2,1)S(1)} %bitcast.2, s32[1,1024]{1,0:T(1,128)S(1)} %copy-done.1, f32[2]{0:T(128)S(1)} %copy-done.2), custom_call_target="tpu_custom_call" | custom-call | tf_op jit(solution)/shard_map/pallas_call | solution.py:471
  44.9 1.3 %copy.7 = f32[1,128,2,2,1024]{4,3,2,1,0:T(2,128)} copy(f32[1,128,2,2,1024]{4,3,2,1,0:T(2,128)S(1)} %bitcast.3) | data formatting | bytes 4194304
  46.3 0.5 %copy.8 = f32[1,128]{1,0:T(1,128)} copy(f32[1,128]{1,0:T(1,128)S(1)} %get-tuple-element.9) | data formatting | bytes 1024
Async XLA Ops:
  0.6 1.6 %copy-start = (bf16[1,2,128,2,2,1024]{5,4,3,2,1,0:T(2,128)(2,1)S(1)}, bf16[1,2,128,2,2,1024]{5,4,3,2,1,0:T(2,128)(2,1)}, u32[]{:S(2)}) copy-start(bf16[1,2,128,2,2,1024]{5,4,3,2,1,0:T(2,128)(2,1)} %param.3) | copy-start | bytes 6291460
  2.2 0.7 %copy-start.1 = (s32[1,1024]{1,0:T(1,128)S(1)}, s32[1,1024]{1,0:T(1,128)}, u32[]{:S(2)}) copy-start(s32[1,1024]{1,0:T(1,128)} %source.1) | copy-start | bytes 12292
  2.9 0.7 %copy-start.2 = (f32[2]{0:T(128)S(1)}, f32[2]{0:T(128)}, u32[]{:S(2)}) copy-start(f32[2]{0:T(128)} %weights.1) | copy-start | bytes 28

commit v2 on v1

--- a/solution.py
+++ b/solution.py
@@ -217,10 +217,12 @@
 def merge_kernel(
     n_energy,
     boundary,
+    source_in,
+    weights_in,
+    out,
+    density,
     source,
     weights,
-    out,
-    density,
     raw,
     picks,
     flat,
@@ -274,6 +276,8 @@
         )
         for part in range(2)
     ]
+    loads.insert(0, pltpu.make_async_copy(source_in, source, load_sem.at[2]))
+    loads.append(pltpu.make_async_copy(weights_in, weights, load_sem.at[3]))
     for load in loads:
         load.start()
     barrier = pltpu.get_barrier_semaphore()
@@ -287,12 +291,13 @@
             device_id_type=pl.DeviceIdType.MESH,
         )
 
+    loads[0].wait()
     wanted = source[...]
     deep = min(256, width)
     for begin in range(0, width, deep):
         node = lax.broadcasted_iota(jnp.int32, (deep, width), 0) + begin
         picks[begin : begin + deep, :] = jnp.where(node == wanted, 1.0, 0.0).astype(jnp.bfloat16)
-    loads[0].wait()
+    loads[1].wait()
     pl.semaphore_wait(barrier, 2 + n_energy)
 
     def rows_of(which):
@@ -340,7 +345,8 @@
     for e in all_e:
         pass_on(core_so, e, right_at(cluster, e, tile), to_core)
 
-    loads[1].wait()
+    loads[2].wait()
+    loads[3].wait()
     put(outer, dot(raw[1], picks[:, :half]))
     put(outer, dot(raw[1], picks[:, half:]), blocks)
 
@@ -474,9 +480,11 @@
             jax.ShapeDtypeStruct((rows, energies, 2, width), f32),
             jax.ShapeDtypeStruct((1, rows), f32),
         ),
-        in_specs=[anywhere, vmem, pl.BlockSpec(memory_space=pltpu.SMEM)],
+        in_specs=[pl.BlockSpec(memory_space=pltpu.HBM)] * 3,
         out_specs=(anywhere, vmem),
         scratch_shapes=[
+            pltpu.VMEM(column_source.shape, jnp.int32),
+            pltpu.SMEM(energy_weights.shape, f32),
             pltpu.VMEM((2, lines, width), bf16),
             pltpu.VMEM((width, width), bf16),
             pltpu.VMEM((half // LANES, lines, LANES), f32),
@@ -488,7 +496,7 @@
             pltpu.VMEM((2, half, half), bf16),
             pltpu.VMEM((energies, 2 * rows, half), bf16),
             pltpu.VMEM((n_energy, 8, rows), f32),
-            pltpu.SemaphoreType.DMA((2,)),
+            pltpu.SemaphoreType.DMA((4,)),
             pltpu.SemaphoreType.DMA((2, half // LANES)),
             pltpu.SemaphoreType.DMA((11, energies)),
             pltpu.SemaphoreType.DMA((11, energies)),
@@ -496,7 +504,7 @@
             pltpu.SemaphoreType.DMA((n_energy,)),
         ],
         compiler_params=pltpu.CompilerParams(
-            collective_id=0, has_side_effects=True, vmem_limit_bytes=48 << 20
+            collective_id=0, has_side_effects=True, vmem_limit_bytes=62 << 20
         ),
     )(boundary[0], column_source, energy_weights)
     return result[None], density

time: 47 us -> 45.3 us (0.964)
  Pallas kernels: 41.4 us -> 40.2 us
  local copies, waits for them, and re-layouts: 4.76 us -> 4.25 us
    pallas_call x1, Pallas kernels: 41.4 us -> 40.2 us  [merge_once(): pl.pallas_call(functools.partial(merge_kernel, n_energy), out_shape=(jax....]
    unnamed x8 -> x4, local copies, waits for them, and re-layouts: 4.76 us -> 4.25 us
where the time goes in v2:
time: 45.3 us; the launch traced here: 45.1 us
  Pallas kernels  40.2 us (89%)
  local copies, waits for them, and re-layouts  4.25 us (9%)
  between operations  0.65 us (1%)
    pallas_call x1, Pallas kernels, merge_once(): pl.pallas_call(functools.partial(merge_kernel, n_energy), out_shape=(jax....  40.2 us
    unnamed x4, local copies, waits for them, and re-layouts  4.25 us

profile of v2, /device:TPU:0, one launch (start us, length us, event | category | flops | bytes accessed | tf_op | source)
XLA Modules:
  0.0 45.1 jit_solution(1107295370802555958)
XLA Ops:
  0.6 40.2 %shard_map.50 = (f32[128,2,2,1024]{3,2,1,0:T(2,128)}, f32[1,128]{1,0:T(1,128)}) custom-call(bf16[2,128,2,2,1024]{4,3,2,1,0:T(2,128)(2,1)} %bitcast.2, s32[1,1024]{1,0:T(1,128)} %source_in.1, f32[2]{0:T(128)} %weights_in.1), custom_call_target="tpu_custom_call" | custom-call | tf_op jit(solution)/shard_map/pallas_call | solution.py:477
  40.8 0.0 copy-start
  40.8 3.7 %copy.7 = f32[1,128,2,2,1024]{4,3,2,1,0:T(2,128)} copy(f32[1,128,2,2,1024]{4,3,2,1,0:T(2,128)} %bitcast.3) | data formatting | bytes 4194304
  44.6 0.0 copy-done
  44.6 0.5 %copy.8 = f32[1,128]{1,0:T(1,128)} copy(f32[1,128]{1,0:T(1,128)S(1)} %copy-done) | data formatting | bytes 1024
Async XLA Ops:
  40.8 3.7 %copy-start = (f32[1,128]{1,0:T(1,128)S(1)}, f32[1,128]{1,0:T(1,128)}, u32[]{:S(2)}) copy-start(f32[1,128]{1,0:T(1,128)} %get-tuple-element.9) | copy-start | bytes 1540
